TPU v7x, 256 devices: a whole 4x4x8 slice. The times are simulated.
256 devices in a mesh: row: 8 (over y, core), col: 32 (over x, z).
Axes of the slice: x: 4, y: 4, z: 8, core: 2. Of those that a mesh axis runs over, the one named last changes fastest.
Arguments:
- pivots: bfloat16 [2, 1024, 128], P(None, ('row', 'col')), may hold values from -4 to 4
- landmarks: bfloat16 [98304, 128], P(('row', 'col')), may hold values from -4 to 4
Outputs:
- low_panel: float32 [98304, 1024], P(('row', 'col'))
- updated_panel: float32 [98304, 1024], P(('row', 'col'))
- next_block: float32 [1024, 1024], P(('row', 'col'))
All inputs are finite; a program needn't handle non-finite values.
Results may differ from a plain program's by a relative error of at most 0.0003.
Values may be sent and summed in bfloat16 or wider, within the bound.
No kernel may reach another device: no remote copies, remote signals or barrier semaphores. Data moves between devices by JAX's collectives and lax.ppermute only.
A program may use at most 128 MiB of HBM per device.

v0:
```python
import jax
import jax.numpy as jnp
from jax import lax
from jax.sharding import PartitionSpec as P

FEAT = 128


ridge = 1.0


def kernel(left_rows, right_rows):
    cross = jnp.dot(left_rows, right_rows.T, preferred_element_type=jnp.float32)
    left_sq = jnp.sum(jnp.square(left_rows.astype(jnp.float32)), axis=1)
    right_sq = jnp.sum(jnp.square(right_rows.astype(jnp.float32)), axis=1)
    return jnp.exp(-(left_sq[:, None] + right_sq[None, :] - 2.0 * cross) / FEAT)


def body(pivots, landmarks):
    own_count = pivots.shape[1]
    local_rows = landmarks.shape[0]
    everyone = lax.all_gather(pivots, ("row", "col"), axis=1, tiled=True)
    width = everyone.shape[1]
    identity = jnp.eye(width, dtype=jnp.float32)
    offset = lax.axis_index(("row", "col")) * own_count
    factor = jnp.linalg.cholesky(kernel(everyone[0], everyone[0]) + ridge * identity)
    own_extra = pivots[1]
    left_rows = jnp.concatenate([landmarks, own_extra], axis=0)
    kernels = kernel(left_rows, everyone.reshape(2 * width, everyone.shape[2]))
    left_kernels = kernels[:, :width]
    inverse = jax.scipy.linalg.solve_triangular(factor, identity, lower=True)
    solved = jnp.dot(left_kernels, inverse.T, precision=lax.Precision.HIGHEST)
    right_kernels = kernels[:, width:]
    pivot_panel = lax.all_gather(solved[local_rows:], ("row", "col"), axis=0, tiled=True)
    products = jnp.dot(solved, pivot_panel.T, precision=lax.Precision.HIGHEST)
    identity_rows = lax.dynamic_slice_in_dim(identity, offset, own_count, 0)
    next_rows = right_kernels[local_rows:] + ridge * identity_rows - products[local_rows:]
    updated = right_kernels[:local_rows] - products[:local_rows]
    return (solved[:local_rows], updated, next_rows)


def solution(mesh):
    in_specs = (P(None, ("row", "col"), None), P(("row", "col"), None))
    out_specs = (P(("row", "col"), None), P(("row", "col"), None), P(("row", "col"), None))
    return jax.shard_map(body, mesh=mesh, in_specs=in_specs, out_specs=out_specs, check_vma=False)
```

profile of v0, /device:TPU:1, one launch (start us, length us, event | category | flops | bytes accessed | tf_op | source)
XLA Modules:
  0.0 601.8 jit_solution(5650595546227168124)
XLA Ops:
  10.0 74.5 %all_gather.6 = bf16[2,1024,128]{2,0,1:T(2,128)(2,1)S(1)} all-gather(bf16[2,4,128]{2,0,1:T(2,128)(2,1)S(1)} %copy.20), channel_id=1, replica_groups=mesh['row'=8,'col'=32] {'row','col'}, dimensions={1}, use_global_device_ids=true | all-gather | bytes 526336 | tf_op jit(solution)/shard_map/all_gather | solution.py:22
  85.9 5.5 broadcast_add_fusion
  91.4 5.4 copy.24
  102.2 6.0 add_multiply_fusion
  110.1 11.7 %cholesky.223 = f32[128,128]{1,0:T(8,128)S(1)} custom-call(f32[128,128]{1,0:T(8,128)S(1)} %cholesky.580), custom_call_target="Cholesky" | custom-call | tf_op jit(solution)/shard_map/jit(cholesky)/cholesky | solution.py:26
  121.9 9.8 %custom-call.63 = f32[1,128,128]{1,2,0:T(8,128)S(1)} custom-call(f32[1,128,128]{2,1,0:T(8,128)S(1)} %get-tuple-element.67), custom_call_target="InvertDiagBlocksLowerTriangular" | custom-call | tf_op jit(solution)/shard_map/jit(cholesky)/cholesky | solution.py:26
  138.1 11.7 %cholesky.244 = f32[128,128]{1,0:T(8,128)S(1)} custom-call(f32[128,128]{1,0:T(8,128)S(1)} %cholesky.584), custom_call_target="Cholesky" | custom-call | tf_op jit(solution)/shard_map/jit(cholesky)/cholesky | solution.py:26
  150.5 10.0 %custom-call.64 = f32[1,128,128]{1,2,0:T(8,128)S(1)} custom-call(f32[1,128,128]{2,1,0:T(8,128)S(1)} %get-tuple-element.64), custom_call_target="InvertDiagBlocksLowerTriangular" | custom-call | tf_op jit(solution)/shard_map/jit(cholesky)/cholesky | solution.py:26
  163.8 11.7 %cholesky.468 = f32[128,128]{1,0:T(8,128)S(1)} custom-call(f32[128,128]{1,0:T(8,128)S(1)} %cholesky.589), custom_call_target="Cholesky" | custom-call | tf_op jit(solution)/shard_map/jit(cholesky)/cholesky | solution.py:26
  176.8 9.8 %custom-call.65 = f32[1,128,128]{1,2,0:T(8,128)S(1)} custom-call(f32[1,128,128]{2,1,0:T(8,128)S(1)} %get-tuple-element.61), custom_call_target="InvertDiagBlocksLowerTriangular" | custom-call | tf_op jit(solution)/shard_map/jit(cholesky)/cholesky | solution.py:26
  190.2 12.1 %cholesky.487 = f32[128,128]{1,0:T(8,128)S(1)} custom-call(f32[128,128]{1,0:T(8,128)S(1)} %cholesky.594), custom_call_target="Cholesky" | custom-call | tf_op jit(solution)/shard_map/jit(cholesky)/cholesky | solution.py:26
  203.6 9.8 %custom-call.66 = f32[1,128,128]{1,2,0:T(8,128)S(1)} custom-call(f32[1,128,128]{2,1,0:T(8,128)S(1)} %get-tuple-element.58), custom_call_target="InvertDiagBlocksLowerTriangular" | custom-call | tf_op jit(solution)/shard_map/jit(cholesky)/cholesky | solution.py:26
  216.9 11.7 %cholesky.506 = f32[128,128]{1,0:T(8,128)S(1)} custom-call(f32[128,128]{1,0:T(8,128)S(1)} %cholesky.599), custom_call_target="Cholesky" | custom-call | tf_op jit(solution)/shard_map/jit(cholesky)/cholesky | solution.py:26
  230.0 9.8 %custom-call.67 = f32[1,128,128]{1,2,0:T(8,128)S(1)} custom-call(f32[1,128,128]{2,1,0:T(8,128)S(1)} %get-tuple-element.55), custom_call_target="InvertDiagBlocksLowerTriangular" | custom-call | tf_op jit(solution)/shard_map/jit(cholesky)/cholesky | solution.py:26
  243.3 11.7 %cholesky.526 = f32[128,128]{1,0:T(8,128)S(1)} custom-call(f32[128,128]{1,0:T(8,128)S(1)} %cholesky.604), custom_call_target="Cholesky" | custom-call | tf_op jit(solution)/shard_map/jit(cholesky)/cholesky | solution.py:26
  256.4 9.8 %custom-call.68 = f32[1,128,128]{1,2,0:T(8,128)S(1)} custom-call(f32[1,128,128]{2,1,0:T(8,128)S(1)} %get-tuple-element.52), custom_call_target="InvertDiagBlocksLowerTriangular" | custom-call | tf_op jit(solution)/shard_map/jit(cholesky)/cholesky | solution.py:26
  269.2 11.7 %cholesky.546 = f32[128,128]{1,0:T(8,128)S(1)} custom-call(f32[128,128]{1,0:T(8,128)S(1)} %cholesky.609), custom_call_target="Cholesky" | custom-call | tf_op jit(solution)/shard_map/jit(cholesky)/cholesky | solution.py:26
  282.2 10.0 %custom-call.69 = f32[1,128,128]{1,2,0:T(8,128)S(1)} custom-call(f32[1,128,128]{2,1,0:T(8,128)S(1)} %get-tuple-element.49), custom_call_target="InvertDiagBlocksLowerTriangular" | custom-call | tf_op jit(solution)/shard_map/jit(cholesky)/cholesky | solution.py:26
  294.9 11.7 %cholesky.564 = f32[128,128]{1,0:T(8,128)S(1)} custom-call(f32[128,128]{1,0:T(8,128)S(1)} %convolution_subtract_fusion.11), custom_call_target="Cholesky" | custom-call | tf_op jit(solution)/shard_map/jit(cholesky)/cholesky | solution.py:26
  318.5 27.5 %while.1 = (s32[]{:T(128)}, f32[1024,1024]{1,0:T(8,128)}, s32[8,2]{0,1:T(2,128)S(1)}, f32[8,128,128]{2,1,0:T(8,128)}, s32[]{:T(128)}) while((s32[]{:T(128)}, f32[1024,1024]{1,0:T(8,128)}, s32[8,2]{0,1:T(2,128)S(1)}, f32[8,128,128]{2,1,0:T(8,128)}, s32[]{:T(128)}) %tuple.63), condition=%wide.while_cond, body=%wide.while_body.sunk | while | flops 2 | bytes 132705 | solution.py:31
  346.0 79.8 %custom-call.70 = f32[8,128,128]{1,2,0:T(8,128)S(1)} custom-call(f32[8,128,128]{2,1,0:T(8,128)} %get-tuple-element.10), custom_call_target="InvertDiagBlocksLowerTriangular" | custom-call | tf_op jit(solution)/shard_map/jit(_solve_triangular)/triangular_solve | solution.py:31
  455.5 8.6 %fusion.9 = f32[388,1024]{1,0:T(8,128)S(1)} fusion(f32[1024,1024]{1,0:T(8,128)} %convolution_dynamic-update-slice_fusion, f32[388,2048]{1,0:T(8,128)S(1)} %multiply_exponential_fusion), kind=kOutput, calls=%fused_computation.19 | convolution fusion | flops 4882169856 | bytes 7389184 | tf_op jit(solution)/shard_map/dot_general | solution.py:32
  466.1 111.8 %all-gather.3.cloned.1.call-done = f32[256,4,1024]{2,1,0:T(4,128)} async-done(((f32[1,4,1024]{2,1,0:T(4,128)}), f32[256,4,1024]{2,1,0:T(4,128)}) %all-gather.3.cloned.1.call-update) | async-done | bytes 4194320 | tf_op jit(solution)/shard_map/all_gather | solution.py:34
  583.1 7.4 %fusion.75 = f32[388,1024]{1,0:T(8,128)S(1)} fusion(f32[388,1024]{1,0:T(8,128)S(1)} %fusion.9, f32[1024,1024]{1,0:T(8,128)} %reshape.115), kind=kOutput, calls=%fused_computation.178 | convolution fusion | flops 4882169856 | bytes 7372800 | tf_op jit(solution)/shard_map/dot_general | solution.py:35
  (109 shorter events, 120.1 us)
Async XLA Ops:
  7.2 2.8 copy-start.4
  7.2 570.7 %all-gather.3.cloned.1.call-start = ((), (), s32[]{:S(2)}) async-start(), calls=%async_computation | async-start | bytes 4210688 | tf_op jit(solution)/shard_map/all_gather | solution.py:34
  108.2 2.0 copy-start.1
  425.8 4.7 copy-start
  448.0 6.5 %copy-start.3 = (bf16[384,128]{1,0:T(8,128)(2,1)S(1)}, bf16[384,128]{1,0:T(8,128)(2,1)}, u32[]{:S(2)}) copy-start(bf16[384,128]{1,0:T(8,128)(2,1)} %param.3) | copy-start | bytes 294916
  455.5 8.7 %copy-start.2 = (f32[388,2048]{1,0:T(8,128)}, f32[388,2048]{1,0:T(8,128)S(1)}, u32[]{:S(2)}) copy-start(f32[388,2048]{1,0:T(8,128)S(1)} %multiply_exponential_fusion) | copy-start | bytes 9535492
Sparse Core Ops, SparseCore 0:
  464.9 112.8 all-gather.2
where the time goes:
time: 608 us; the launch traced here: 602 us
  other arithmetic  271 us (45%)
  waiting for transfers between devices  112 us (18%)
  blocking collectives  74.5 us (12%)
  matrix products  74.2 us (12%)
  local copies, waits for them, and re-layouts  50.1 us (8%)
  between operations  19.7 us (3%)
    another operation x30, other arithmetic, body(): jnp.linalg.cholesky(kernel(everyone[0], everyone[0]) + ridge * identity)  172 us
    all_gather x1, waiting for transfers between devices, body(): lax.all_gather(solved[local_rows:], ('row', 'col'), axis=0, tiled=True)  112 us
    another operation x3, other arithmetic, body(): inverse = jax.scipy.linalg.solve_triangular(factor, identity, lower=True)  84.6 us
    all_gather x1, blocking collectives, body(): everyone = lax.all_gather(pivots, ('row', 'col'), axis=1, tiled=True)  74.5 us
    another operation x15, matrix products, body(): inverse = jax.scipy.linalg.solve_triangular(factor, identity, lower=True)  28.5 us
    another operation x24, local copies, waits for them, and re-layouts  27.5 us
    another operation x14, matrix products, body(): jnp.linalg.cholesky(kernel(everyone[0], everyone[0]) + ridge * identity)  23.3 us
  transfers between devices with their start and end apart: 1, of which 1 were waited for; matrix products, arithmetic and copies ran while one was open for 0% of the time, Pallas kernels for 0%

commit v1 on v0

v1 whole, which is shorter than its diff:
```python
import jax
import jax.numpy as jnp
from jax import lax
from jax.experimental import pallas as pl
from jax.experimental.pallas import tpu as pltpu
from jax.sharding import PartitionSpec as P

FEAT = 128
PANEL = 1024
RIDGE = 1.0
SUB = 8
LANES = 128
INNER = 128
OUTER = 256
f32 = jnp.float32
bf16 = jnp.bfloat16


def split(x):
    high = x.astype(bf16)
    return high, (x - high.astype(f32)).astype(bf16)


def dot_t(a, b):
    return lax.dot_general(a, b, (((1,), (1,)), ((), ())), preferred_element_type=f32)


def dot_n(a, b):
    return jnp.dot(a, b, preferred_element_type=f32)


def product(dot, a, b):
    return dot(a[0], b[0]) + (dot(a[0], b[1]) + dot(a[1], b[0]))


def over_lanes(x, column):
    return jnp.broadcast_to(x[:, column:column + 1], (SUB, LANES))


def over_rows(x, row):
    return jnp.broadcast_to(x[row:row + 1, :], (SUB, LANES))


def inverse_factor(block):
    rows_in_tile = lax.broadcasted_iota(jnp.int32, (SUB, LANES), 0)
    lane = lax.broadcasted_iota(jnp.int32, (SUB, LANES), 1)
    tiles = INNER // SUB
    rows = [block[SUB * t:SUB * (t + 1), :] for t in range(tiles)]
    found = []
    for t in range(tiles):
        first = SUB * t
        columns = [over_lanes(rows[t], first + m) for m in range(SUB)]
        here = (lane >= first) & (lane < first + SUB)
        current = jnp.where(here, jnp.where(lane - first == rows_in_tile, 1.0, 0.0), rows[t])
        scaled = jnp.zeros((SUB, LANES), f32)
        for k in range(SUB):
            pivot = over_rows(columns[k], k)
            inverse = 1.0 / pivot
            pivot_row = over_rows(current, k)
            scaled = jnp.where(rows_in_tile == k, pivot_row * lax.rsqrt(pivot), scaled)
            factors = jnp.where(rows_in_tile == k, 1.0 - inverse, columns[k] * inverse)
            current = current - factors * pivot_row
            for m in range(k + 1, SUB):
                columns[m] = columns[m] - factors * over_rows(columns[m], k)
        found.append(jnp.where(lane <= first + rows_in_tile, scaled, 0.0))
        pivots = [over_rows(current, m) for m in range(SUB)]
        for s in range(t + 1, tiles):
            terms = [over_lanes(rows[s], first + m) * pivots[m] for m in range(SUB)]
            while len(terms) > 1:
                terms = [a + b for a, b in zip(terms[::2], terms[1::2])]
            rows[s] = jnp.where(here, 0.0, rows[s]) - terms[0]
    return jnp.concatenate(found, axis=0)


def squares(x):
    x = x.astype(f32)
    return jnp.sum(x * x, axis=1, keepdims=True)


def squares_along_lanes(x):
    x = x.astype(f32)
    high, low = split(x * x)
    ones = jnp.ones((16, FEAT), bf16)
    return (dot_t(ones, high) + dot_t(ones, low))[:1]


def kernel_values(left, left_sq, right, right_sq):
    return jnp.exp((2.0 * dot_t(left, right) - left_sq - right_sq) * (1.0 / FEAT))


def local_body(local_rows, pivots_ref, left_ref, low_ref, updated_ref, next_ref,
               panel, bottom, panel_high, panel_low, bottom_high, bottom_low, right_kernels):
    own_rows = next_ref.shape[0]
    offset = lax.axis_index(("row", "col")) * own_rows
    left_count = left_ref.shape[0]
    first = pivots_ref[:PANEL, :]
    first_lanes = squares_along_lanes(first)
    chunk = OUTER
    chunks = [(at, chunk) for at in range(0, PANEL, chunk)]
    bottom_chunks = chunks + [(PANEL, left_count)]

    def rows_of(at, count):
        return left_ref[...] if at == PANEL else pivots_ref[pl.ds(PANEL + at, count), :]

    for at, count in chunks:
        x = pivots_ref[at:at + count, :]
        values = kernel_values(x, squares(x), first, first_lanes)
        row = lax.broadcasted_iota(jnp.int32, values.shape, 0) + at
        column = lax.broadcasted_iota(jnp.int32, values.shape, 1)
        panel[at:at + count, :] = values + jnp.where(row == column, RIDGE, 0.0)
    for at, count in bottom_chunks:
        x = rows_of(at, count)
        bottom[at:at + count, :] = kernel_values(x, squares(x), first, first_lanes)
    second = pivots_ref[PANEL:, :]
    x = left_ref[...]
    right_kernels[...] = kernel_values(x, squares(x), second, squares_along_lanes(second))

    for step in range(PANEL // OUTER):
        at = step * OUTER
        columns = slice(at, at + OUTER)
        mid = at + INNER
        end = at + OUTER
        if step:
            right = (panel_high[columns, :at], panel_low[columns, :at])
            for start, count in chunks[step:]:
                rows = slice(start, start + count)
                left = (panel_high[rows, :at], panel_low[rows, :at])
                panel[rows, columns] = panel[rows, columns] - product(dot_t, left, right)
            for start, count in bottom_chunks:
                rows = slice(start, start + count)
                left = (bottom_high[rows, :at], bottom_low[rows, :at])
                bottom[rows, columns] = bottom[rows, columns] - product(dot_t, left, right)
        upper = inverse_factor(panel[at:mid, at:mid])
        upper_parts = split(upper)
        across = product(dot_t, split(panel[mid:end, at:mid]), upper_parts)
        across_parts = split(across)
        lower = inverse_factor(panel[mid:end, mid:end] - product(dot_t, across_parts, across_parts))
        corner = -product(dot_n, split(lower), split(product(dot_n, across_parts, upper_parts)))
        inverse = jnp.concatenate([
            jnp.concatenate([upper, jnp.zeros((INNER, INNER), f32)], axis=1),
            jnp.concatenate([corner, lower], axis=1)], axis=0)
        inverse = split(inverse)
        for start, count in chunks[step + 1:]:
            rows = slice(start, start + count)
            solved = product(dot_t, split(panel[rows, columns]), inverse)
            panel_high[rows, columns], panel_low[rows, columns] = split(solved)
        for start, count in bottom_chunks:
            rows = slice(start, start + count)
            solved = product(dot_t, split(bottom[rows, columns]), inverse)
            bottom_high[rows, columns], bottom_low[rows, columns] = split(solved)
            if start == PANEL:
                low_ref[:, columns] = solved[:local_rows]

    left = (bottom_high[PANEL:, :], bottom_low[PANEL:, :])
    for start, count in chunks:
        rows = slice(start, start + count)
        right = (bottom_high[rows, :], bottom_low[rows, :])
        values = right_kernels[:, rows] - product(dot_t, left, right)
        updated_ref[:, rows] = values[:local_rows]
        own = values[local_rows:local_rows + own_rows]
        row = lax.broadcasted_iota(jnp.int32, own.shape, 0) + offset
        column = lax.broadcasted_iota(jnp.int32, own.shape, 1) + start
        next_ref[:, rows] = own + jnp.where(row == column, RIDGE, 0.0)


def local_call(pivots, left, local_rows, own_rows):
    left_count = left.shape[0]
    body = lambda *refs: local_body(local_rows, *refs)
    total = PANEL + left_count
    return pl.pallas_call(
        body,
        out_shape=(
            jax.ShapeDtypeStruct((local_rows, PANEL), f32),
            jax.ShapeDtypeStruct((local_rows, PANEL), f32),
            jax.ShapeDtypeStruct((own_rows, PANEL), f32),
        ),
        scratch_shapes=[
            pltpu.VMEM((PANEL, PANEL), f32),
            pltpu.VMEM((total, PANEL), f32),
            pltpu.VMEM((PANEL, PANEL), bf16),
            pltpu.VMEM((PANEL, PANEL), bf16),
            pltpu.VMEM((total, PANEL), bf16),
            pltpu.VMEM((total, PANEL), bf16),
            pltpu.VMEM((left_count, PANEL), f32),
        ],
        compiler_params=pltpu.CompilerParams(vmem_limit_bytes=56 * 1024 * 1024),
        name="panels",
    )(pivots, left)


def body(pivots, landmarks):
    axes = ("row", "col")
    devices = lax.axis_size(axes)
    own_count, feat = pivots.shape[1:]
    local_rows = landmarks.shape[0]
    copies = jnp.broadcast_to(pivots[None], (devices,) + pivots.shape)
    gathered = lax.all_to_all(copies, axes, 0, 0, tiled=True)
    everyone = gathered.transpose(1, 0, 2, 3).reshape(2 * devices * own_count, feat)
    padding = jnp.zeros((16 - own_count, feat), landmarks.dtype)
    left = jnp.concatenate([landmarks, pivots[1], padding], axis=0)
    return local_call(everyone, left, local_rows, own_count)


def solution(mesh):
    in_specs = (P(None, ("row", "col"), None), P(("row", "col"), None))
    out_specs = (P(("row", "col"), None), P(("row", "col"), None), P(("row", "col"), None))
    return jax.shard_map(body, mesh=mesh, in_specs=in_specs, out_specs=out_specs, check_vma=False)
```

time: 608 us -> 90.9 us (0.15)
  other arithmetic: 271 us -> 0.76 us
  waiting for transfers between devices: 112 us -> 20.5 us
  blocking collectives: 74.5 us -> 0 us
  matrix products: 74.2 us -> 0 us
  Pallas kernels: 0 us -> 50.4 us
  local copies, waits for them, and re-layouts: 50.1 us -> 2.73 us
  between operations: 19.7 us -> 0.67 us
  starting transfers between devices: 0.04 us -> 15.7 us
    another operation x33 -> x0, other arithmetic: 257 us -> none  [the longest x30 172 us: body(): jnp.linalg.cholesky(kernel(everyone[0], everyone[0]) + ridge * identity)]
    all_gather x1 -> x0, waiting for transfers between devices: 112 us -> none  [body(): lax.all_gather(solved[local_rows:], ('row', 'col'), axis=0, tiled=True)]
    all_gather x1 -> x0, blocking collectives: 74.5 us -> none  [body(): everyone = lax.all_gather(pivots, ('row', 'col'), axis=1, tiled=True)]
    another operation x29 -> x0, matrix products: 51.8 us -> none  [the longest x15 28.5 us: body(): inverse = jax.scipy.linalg.solve_triangular(factor, identity, lower=True)]
    pallas_call x0 -> x1, Pallas kernels: none -> 50.4 us  [local_call(): pl.pallas_call(body, out_shape=(jax.ShapeDtypeStruct((local_rows, PANEL),...]
    another operation x33 -> x0, local copies, waits for them, and re-layouts: 30 us -> none
    dot_general x4 -> x0, matrix products: 22.5 us -> none  [the longest x1 8.65 us: body(): solved = jnp.dot(left_kernels, inverse.T, precision=lax.Precision.HIGHEST)]
    all_to_all x0 -> x1, waiting for transfers between devices: none -> 20.5 us  [body(): gathered = lax.all_to_all(copies, axes, 0, 0, tiled=True)]
  transfers between devices with their start and end apart: 1 -> 1, of which waited for: 1 -> 1; matrix products, arithmetic and copies ran while one was open for 0% -> 1% of each run, Pallas kernels for 0% -> 0%
where the time goes in v1:
time: 90.9 us; the launch traced here: 90.7 us
  Pallas kernels  50.4 us (55%)
  waiting for transfers between devices  20.5 us (23%)
  starting transfers between devices  15.7 us (17%)
  local copies, waits for them, and re-layouts  2.73 us (3%)
    pallas_call x1, Pallas kernels, local_call(): pl.pallas_call(body, out_shape=(jax.ShapeDtypeStruct((local_rows, PANEL),...  50.4 us
    all_to_all x1, waiting for transfers between devices, body(): gathered = lax.all_to_all(copies, axes, 0, 0, tiled=True)  20.5 us
    all_to_all x1, starting transfers between devices, body(): gathered = lax.all_to_all(copies, axes, 0, 0, tiled=True)  15.7 us
  transfers between devices with their start and end apart: 1, of which 1 were waited for; matrix products, arithmetic and copies ran while one was open for 1% of the time, Pallas kernels for 0%

profile of v1, /device:TPU:1, one launch (start us, length us, event | category | flops | bytes accessed | tf_op | source)
XLA Modules:
  0.0 90.7 jit_solution(17018195284429262929)
XLA Ops:
  0.6 0.0 copy-start.1
  0.6 0.0 copy-start
  0.6 1.7 %broadcast_in_dim.4 = bf16[256,2,4,128]{3,2,1,0:T(4,128)(2,1)} broadcast(bf16[2,4,128]{2,1,0:T(4,128)(2,1)} %param.2), dimensions={1,2,3} | broadcast | bytes 526336 | tf_op jit(solution)/shard_map/broadcast_in_dim | solution.py:196
  2.3 15.7 %all-to-all-start = ((bf16[256,2,4,128]{3,2,1,0:T(4,128)(2,1)}), bf16[256,2,4,128]{3,2,1,0:T(4,128)(2,1)S(1)}, u32[]{:S(2)}, u32[]{:S(2)}) async-start(bf16[256,2,4,128]{3,2,1,0:T(4,128)(2,1)} %broadcast_in_dim.4), calls=%async_computation | async-start | bytes 1048576 | tf_op jit(solution)/shard_map/all_to_all | solution.py:197
  18.0 0.1 pad.2.clone
  18.1 0.0 copy-done.1
  18.1 0.0 copy-done
  18.1 0.8 maximum_maximum_fusion.refs_1_
  18.8 20.5 %all-to-all-done = bf16[256,2,4,128]{3,2,1,0:T(4,128)(2,1)S(1)} async-done(((bf16[256,2,4,128]{3,2,1,0:T(4,128)(2,1)}), bf16[256,2,4,128]{3,2,1,0:T(4,128)(2,1)S(1)}, u32[]{:S(2)}, u32[]{:S(2)}) %all-to-all-start) | async-done | bytes 524320 | tf_op jit(solution)/shard_map/all_to_all | solution.py:197
  39.4 1.0 %copy.5 = bf16[2,256,4,128]{3,2,1,0:T(4,128)(2,1)} copy(bf16[2,256,4,128]{3,2,0,1:T(4,128)(2,1)S(1)} %bitcast.4) | data formatting | bytes 1048576 | tf_op jit(solution)/shard_map/transpose | solution.py:198
  40.3 50.4 %panels.1 = (f32[384,1024]{1,0:T(8,128)}, f32[384,1024]{1,0:T(8,128)}, f32[4,1024]{1,0:T(4,128)}) custom-call(bf16[2048,128]{1,0:T(8,128)(2,1)} %bitcast.5, bf16[400,128]{1,0:T(8,128)(2,1)} %maximum_maximum_fusion.refs_1_), custom_call_target="tpu_custom_call" | custom-call | tf_op jit(solution)/shard_map/panels/pallas_call | solution.py:170
  (2 shorter events, 0.0 us)
Async XLA Ops:
  0.6 17.4 %copy-start.1 = (bf16[2,4,128]{2,1,0:T(4,128)(2,1)S(1)}, bf16[2,4,128]{2,1,0:T(4,128)(2,1)}, u32[]{:S(2)}) copy-start(bf16[2,4,128]{2,1,0:T(4,128)(2,1)} %param.2) | copy-start | bytes 6148
  0.6 17.4 %copy-start = (bf16[384,128]{1,0:T(8,128)(2,1)S(1)}, bf16[384,128]{1,0:T(8,128)(2,1)}, u32[]{:S(2)}) copy-start(bf16[384,128]{1,0:T(8,128)(2,1)} %param.3) | copy-start | bytes 294916
  2.3 37.0 %all-to-all-start = ((bf16[256,2,4,128]{3,2,1,0:T(4,128)(2,1)}), bf16[256,2,4,128]{3,2,1,0:T(4,128)(2,1)S(1)}, u32[]{:S(2)}, u32[]{:S(2)}) async-start(bf16[256,2,4,128]{3,2,1,0:T(4,128)(2,1)} %broadcast_in_dim.4), calls=%async_computation | async-start | bytes 1048576 | tf_op jit(solution)/shard_map/all_to_all | solution.py:197

commit v2 on v1

v2 whole, which is shorter than its diff:
```python
import jax
import jax.numpy as jnp
from jax import lax
from jax.experimental import pallas as pl
from jax.experimental.pallas import tpu as pltpu
from jax.sharding import PartitionSpec as P

FEAT = 128
PANEL = 1024
RIDGE = 1.0
SUB = 8
LANES = 128
INNER = 128
OUTER = 256
WINDOW = 4
NEAR = 3
CORES = 2
f32 = jnp.float32
bf16 = jnp.bfloat16


def split(x):
    high = x.astype(bf16)
    return high, (x - high.astype(f32)).astype(bf16)


def dot_t(a, b):
    return lax.dot_general(a, b, (((1,), (1,)), ((), ())), preferred_element_type=f32)


def dot_n(a, b):
    return jnp.dot(a, b, preferred_element_type=f32)


def product(dot, a, b):
    return dot(a[0], b[0]) + (dot(a[0], b[1]) + dot(a[1], b[0]))


def over_lanes(x, column):
    return jnp.broadcast_to(x[:, column:column + 1], (SUB, LANES))


def over_rows(x, row):
    return jnp.broadcast_to(x[row:row + 1, :], (SUB, LANES))


def total_of(terms):
    terms = list(terms)
    while len(terms) > 1:
        terms = [a + b for a, b in zip(terms[::2], terms[1::2])] + terms[len(terms) // 2 * 2:]
    return terms[0]


def inverse_factor(block, work=()):
    work = list(work)
    rows_in_tile = lax.broadcasted_iota(jnp.int32, (SUB, LANES), 0)
    lane = lax.broadcasted_iota(jnp.int32, (SUB, LANES), 1)
    is_row = [rows_in_tile == k for k in range(SUB)]
    tiles = INNER // SUB
    rows = [block[SUB * t:SUB * (t + 1), :] for t in range(tiles)]
    found = []
    pivots = [over_lanes(rows[0], m) for m in range(SUB)]
    share = len(work) / tiles
    done = 0
    for t in range(tiles):
        first = SUB * t
        after = first + SUB
        last = t == tiles - 1
        opened = t // WINDOW * WINDOW
        limit = opened + WINDOW + NEAR
        limit = tiles if limit + 1 >= tiles else limit
        if not last:
            following = [over_lanes(rows[t], after + m) for m in range(SUB)]
            below = [over_lanes(rows[t + 1], first + m) for m in range(SUB)]
            coming = [over_lanes(rows[t + 1], after + m) for m in range(SUB)]
        here = (lane >= first) & (lane < after)
        current = jnp.where(here, jnp.where(lane - first == rows_in_tile, 1.0, 0.0), rows[t])
        scaled = None
        for k in range(SUB):
            pivot = over_rows(pivots[k], k)
            inverse = 1.0 / pivot
            column = jnp.where(is_row[k], -1.0, pivots[k])
            for m in range(k + 1, SUB):
                row = over_rows(pivots[m], k)
                pivots[m] = jnp.where(is_row[k], 0.0, pivots[m]) - (column * row) * inverse
            factors = column * inverse
            row = over_rows(current, k)
            taken = row * lax.rsqrt(pivot)
            scaled = taken if scaled is None else jnp.where(rows_in_tile >= k, taken, scaled)
            current = jnp.where(is_row[k], 0.0, current) - factors * row
            if not last:
                for m in range(SUB):
                    row = over_rows(following[m], k)
                    following[m] = jnp.where(is_row[k], 0.0, following[m]) - factors * row
        found.append(scaled)
        while done < min(len(work), round((t + 1) * share)):
            work[done]()
            done += 1
        if last:
            break
        pivots = [coming[m] - total_of([below[i] * over_rows(following[m], i) for i in range(SUB)])
                  for m in range(SUB)]
        spread = [over_rows(current, m) for m in range(SUB)]
        for s in range(t + 1, limit):
            columns = below if s == t + 1 else [over_lanes(rows[s], first + m) for m in range(SUB)]
            rows[s] = jnp.where(here, 0.0, rows[s]) - total_of(
                [columns[m] * spread[m] for m in range(SUB)])
        if (t + 1) % WINDOW == 0 and limit < tiles:
            window = jnp.concatenate(found[opened:], axis=0)
            rank = lax.broadcasted_iota(jnp.int32, window.shape, 0) + SUB * opened
            place = lax.broadcasted_iota(jnp.int32, window.shape, 1)
            left = split(window.T[SUB * limit:, :])
            window = jnp.where((place > rank) & (place < after), 0.0, window)
            change = product(dot_n, left, split(window))
            inside = (lane >= SUB * opened) & (lane < after)
            for s in range(limit, tiles):
                at = SUB * (s - limit)
                rows[s] = jnp.where(inside, 0.0, rows[s]) - change[at:at + SUB, :]
    return jnp.concatenate([jnp.where(lane <= SUB * t + rows_in_tile, x, 0.0)
                            for t, x in enumerate(found)], axis=0)


def squares(x):
    x = x.astype(f32)
    return jnp.sum(x * x, axis=1, keepdims=True)


def squares_along_lanes(x):
    x = x.astype(f32)
    high, low = split(x * x)
    ones = jnp.ones((16, FEAT), bf16)
    return (dot_t(ones, high) + dot_t(ones, low))[:1]


def kernel_values(left, left_sq, right, right_sq):
    return jnp.exp((2.0 * dot_t(left, right) - left_sq - right_sq) * (1.0 / FEAT))


def arrange_pivots(source_ref, pivots_ref, core):
    chips = lax.axis_size("row") // CORES
    columns = source_ref.shape[0] // chips
    count = columns * SUB // 2
    row = lax.broadcasted_iota(jnp.int32, (columns // 2, SUB, FEAT), 1)
    for y in range(chips):
        x = source_ref[columns * y:columns * (y + 1)].astype(f32).reshape(columns // 2, 2, SUB, FEAT)
        even, odd = x[:, 0], x[:, 1]
        first = jnp.where(row < SUB // 2, even, pltpu.roll(odd, SUB // 2, 1))
        second = jnp.where(row < SUB // 2, pltpu.roll(even, SUB // 2, 1), odd)
        at = (y * CORES + core) * count
        for base, value in ((0, first), (PANEL, second)):
            rows = pl.ds(pl.multiple_of(base + at, count), count)
            pivots_ref[rows, :] = value.reshape(count, FEAT).astype(bf16)


def local_body(own_ref, same_ref, other_ref, landmarks_ref, low_ref, updated_ref, next_ref,
               panel, bottom, panel_high, panel_low, bottom_high, bottom_low, right_kernels,
               inverse_high, inverse_low, pivots_ref, left_ref):
    local_rows = landmarks_ref.shape[0]
    own_rows = next_ref.shape[0]
    offset = lax.axis_index(("row", "col")) * own_rows
    core = lax.axis_index("row") % CORES
    arrange_pivots(same_ref, pivots_ref, core)
    arrange_pivots(other_ref, pivots_ref, 1 - core)
    left_count = left_ref.shape[0]
    left_ref[:local_rows, :] = landmarks_ref[...]
    padding = jnp.zeros((left_count - local_rows - own_rows, FEAT), f32)
    left_ref[local_rows:, :] = jnp.concatenate(
        [own_ref[1].astype(f32), padding], axis=0).astype(bf16)
    first = pivots_ref[:PANEL, :]
    first_lanes = squares_along_lanes(first)
    chunks = [slice(at, at + OUTER) for at in range(0, PANEL, OUTER)]
    part = OUTER
    bottom_chunks = [slice(at, at + part) for at in range(0, PANEL, part)]
    bottom_chunks.append(slice(PANEL, PANEL + left_count))

    def panel_values(rows):
        x = pivots_ref[rows, :]
        width = rows.stop
        values = kernel_values(x, squares(x), first[:width], first_lanes[:, :width])
        row = lax.broadcasted_iota(jnp.int32, values.shape, 0) + rows.start
        column = lax.broadcasted_iota(jnp.int32, values.shape, 1)
        panel[rows, :width] = values + jnp.where(row == column, RIDGE, 0.0)

    def bottom_values(rows):
        x = left_ref[...] if rows.start == PANEL else pivots_ref[PANEL + rows.start:PANEL + rows.stop, :]
        bottom[rows, :] = kernel_values(x, squares(x), first, first_lanes)

    def right_values(columns):
        x = left_ref[...]
        y = pivots_ref[PANEL + columns.start:PANEL + columns.stop, :]
        right_kernels[:, columns] = kernel_values(x, squares(x), y, squares_along_lanes(y))

    def solve(source, high, low, rows, columns):
        inverse = (inverse_high[...], inverse_low[...])
        solved = product(dot_t, split(source[rows, columns]), inverse)
        high[rows, columns], low[rows, columns] = split(solved)
        if rows.start == PANEL:
            low_ref[:, columns] = solved[:local_rows]

    def reduce(target, high, low, rows, columns):
        done = slice(0, columns.start)
        right = (panel_high[columns, done], panel_low[columns, done])
        left = (high[rows, done], low[rows, done])
        target[rows, columns] = target[rows, columns] - product(dot_t, left, right)

    def update(at, columns):
        left = (bottom_high[PANEL:, at], bottom_low[PANEL:, at])
        right = (bottom_high[columns, at], bottom_low[columns, at])
        values = right_kernels[:, columns] - product(dot_t, left, right)
        if at.stop < PANEL:
            right_kernels[:, columns] = values
            return
        updated_ref[:, columns] = values[:local_rows]
        own = values[local_rows:local_rows + own_rows]
        row = lax.broadcasted_iota(jnp.int32, own.shape, 0) + offset
        column = lax.broadcasted_iota(jnp.int32, own.shape, 1) + columns.start
        next_ref[:, columns] = own + jnp.where(row == column, RIDGE, 0.0)

    def later(call, *operands):
        return lambda: call(*operands)

    panel_values(chunks[0])
    for step, columns in enumerate(chunks):
        at, mid, end = columns.start, columns.start + INNER, columns.stop
        work = []
        if step == 0:
            work += [later(panel_values, rows) for rows in chunks[1:]]
            work += [later(bottom_values, rows) for rows in bottom_chunks]
            work += [later(right_values, block) for block in chunks]
        else:
            before = chunks[step - 1]
            reduce(panel, panel_high, panel_low, columns, columns)
            work += [later(solve, panel, panel_high, panel_low, rows, before)
                     for rows in chunks[step + 1:]]
            work += [later(reduce, panel, panel_high, panel_low, rows, columns)
                     for rows in chunks[step + 1:]]
            work += [later(solve, bottom, bottom_high, bottom_low, rows, before)
                     for rows in bottom_chunks]
            work += [later(update, before, block) for block in chunks]
            work += [later(reduce, bottom, bottom_high, bottom_low, rows, columns)
                     for rows in bottom_chunks]
        half = len(work) // 2
        upper = inverse_factor(panel[at:mid, at:mid], work[:half])
        upper_parts = split(upper)
        across = product(dot_t, split(panel[mid:end, at:mid]), upper_parts)
        across_parts = split(across)
        lower = inverse_factor(
            panel[mid:end, mid:end] - product(dot_t, across_parts, across_parts), work[half:])
        corner = -product(dot_n, split(lower), split(product(dot_n, across_parts, upper_parts)))
        inverse = jnp.concatenate([
            jnp.concatenate([upper, jnp.zeros((INNER, INNER), f32)], axis=1),
            jnp.concatenate([corner, lower], axis=1)], axis=0)
        inverse_high[...], inverse_low[...] = split(inverse)
        if step + 1 < len(chunks):
            solve(panel, panel_high, panel_low, chunks[step + 1], columns)
    for rows in bottom_chunks:
        solve(bottom, bottom_high, bottom_low, rows, chunks[-1])
    for block in chunks:
        update(chunks[-1], block)


def local_call(own, same, other, landmarks):
    own_rows = own.shape[1]
    local_rows = landmarks.shape[0]
    left_count = local_rows + 2 * SUB
    total = PANEL + left_count
    return pl.pallas_call(
        local_body,
        out_shape=(
            jax.ShapeDtypeStruct((local_rows, PANEL), f32),
            jax.ShapeDtypeStruct((local_rows, PANEL), f32),
            jax.ShapeDtypeStruct((own_rows, PANEL), f32),
        ),
        scratch_shapes=[
            pltpu.VMEM((PANEL, PANEL), f32),
            pltpu.VMEM((total, PANEL), f32),
            pltpu.VMEM((PANEL, PANEL), bf16),
            pltpu.VMEM((PANEL, PANEL), bf16),
            pltpu.VMEM((total, PANEL), bf16),
            pltpu.VMEM((total, PANEL), bf16),
            pltpu.VMEM((left_count, PANEL), f32),
            pltpu.VMEM((OUTER, OUTER), bf16),
            pltpu.VMEM((OUTER, OUTER), bf16),
            pltpu.VMEM((2 * PANEL, FEAT), bf16),
            pltpu.VMEM((left_count, FEAT), bf16),
        ],
        compiler_params=pltpu.CompilerParams(vmem_limit_bytes=56 * 1024 * 1024),
        name="panels",
    )(own, same, other, landmarks)


def body(pivots, landmarks):
    own_count, feat = pivots.shape[1:]
    rows, columns = lax.axis_size("row"), lax.axis_size("col")
    chips = rows // CORES
    own = pivots.reshape(2 * own_count, feat)
    groups = [[(y * CORES + core) * columns + c for y in range(chips) for c in range(columns)]
              for core in range(CORES)]
    copies = jnp.broadcast_to(own[None], (chips * columns,) + own.shape)
    same = lax.all_to_all(copies, ("row", "col"), 0, 0, axis_index_groups=groups, tiled=True)
    other = lax.ppermute(same, "row", [(i, i ^ 1) for i in range(rows)])
    return local_call(pivots, same, other, landmarks)


def solution(mesh):
    in_specs = (P(None, ("row", "col"), None), P(("row", "col"), None))
    out_specs = (P(("row", "col"), None), P(("row", "col"), None), P(("row", "col"), None))
    return jax.shard_map(body, mesh=mesh, in_specs=in_specs, out_specs=out_specs, check_vma=False)
```

time: 90.9 us -> 70.8 us (0.78)
  blocking collectives: 0 us -> 29.6 us
  waiting for transfers between devices: 20.5 us -> 1.16 us
  Pallas kernels: 50.4 us -> 35.3 us
  starting transfers between devices: 15.7 us -> 2.56 us
  local copies, waits for them, and re-layouts: 2.73 us -> 1.43 us
    all_to_all x0 -> x1, blocking collectives: none -> 29.6 us  [body(): lax.all_to_all(copies, ('row', 'col'), 0, 0, axis_index_groups=groups, ti...]
    all_to_all x1 -> x0, waiting for transfers between devices: 20.5 us -> none  [body(): gathered = lax.all_to_all(copies, axes, 0, 0, tiled=True)]
    all_to_all x1 -> x0, starting transfers between devices: 15.7 us -> none  [body(): gathered = lax.all_to_all(copies, axes, 0, 0, tiled=True)]
    pallas_call x1, Pallas kernels: 50.4 us -> 35.3 us  [local_call(): pl.pallas_call(local_body, out_shape=(jax.ShapeDtypeStruct((local_rows, P...]
    ppermute x0 -> x1, starting transfers between devices: none -> 2.56 us  [body(): other = lax.ppermute(same, 'row', [(i, i ^ 1) for i in range(rows)])]
    ppermute x0 -> x1, waiting for transfers between devices: none -> 1.16 us  [body(): other = lax.ppermute(same, 'row', [(i, i ^ 1) for i in range(rows)])]
    transpose x1 -> x0, local copies, waits for them, and re-layouts: 0.97 us -> none  [body(): gathered.transpose(1, 0, 2, 3).reshape(2 * devices * own_count, feat)]
    broadcast_in_dim x2 -> x1, local copies, waits for them, and re-layouts: 1.67 us -> 0.72 us  [body(): copies = jnp.broadcast_to(own[None], (chips * columns,) + own.shape)]
  transfers between devices with their start and end apart: 1 -> 1, of which waited for: 1 -> 1; matrix products, arithmetic and copies ran while one was open for 1% -> 0% of each run, Pallas kernels for 0% -> 0%
where the time goes in v2:
time: 70.8 us; the launch traced here: 70.7 us
  Pallas kernels  35.3 us (50%)
  blocking collectives  29.6 us (42%)
  starting transfers between devices  2.56 us (4%)
  local copies, waits for them, and re-layouts  1.43 us (2%)
  waiting for transfers between devices  1.16 us (2%)
    pallas_call x1, Pallas kernels, local_call(): pl.pallas_call(local_body, out_shape=(jax.ShapeDtypeStruct((local_rows, P...  35.3 us
    all_to_all x1, blocking collectives, body(): lax.all_to_all(copies, ('row', 'col'), 0, 0, axis_index_groups=groups, ti...  29.6 us
    ppermute x1, starting transfers between devices, body(): other = lax.ppermute(same, 'row', [(i, i ^ 1) for i in range(rows)])  2.56 us
  transfers between devices with their start and end apart: 1, of which 1 were waited for; matrix products, arithmetic and copies ran while one was open for 0% of the time, Pallas kernels for 0%

profile of v2, /device:TPU:1, one launch (start us, length us, event | category | flops | bytes accessed | tf_op | source)
XLA Modules:
  0.0 70.7 jit_solution(8294995577093353122)
XLA Ops:
  0.6 0.7 %broadcast_in_dim.8 = bf16[128,8,128]{2,1,0:T(8,128)(2,1)S(1)} broadcast(bf16[8,128]{1,0:T(8,128)(2,1)} %bitcast.1), dimensions={1,2} | broadcast | bytes 264192 | tf_op jit(solution)/shard_map/broadcast_in_dim | solution.py:299
  1.4 29.6 %all_to_all.5.same_ref = bf16[128,8,128]{2,1,0:T(8,128)(2,1)S(1)} all-to-all(bf16[128,8,128]{2,1,0:T(8,128)(2,1)S(1)} %broadcast_in_dim.8), channel_id=1, replica_groups={{0,1,2,3,4,5,6,7,8,9,10,11,12,13,14,15,16,17,18,19,20,21,22,23,24,25,26..., dimensions={0} | all-to-all | bytes 524288 | tf_op jit(solution)/shard_map/all_to_all | solution.py:300
  31.0 0.0 copy-start
  31.0 2.6 %collective-permute-start = (bf16[128,8,128]{2,1,0:T(8,128)(2,1)S(1)}, bf16[128,8,128]{2,1,0:T(8,128)(2,1)S(1)}, u32[]{:S(2)}, u32[]{:S(2)}) collective-permute-start(bf16[128,8,128]{2,1,0:T(8,128)(2,1)S(1)} %all_to_all.5.same_ref), channel_id=1, source_target_pairs={{0,32},{32,0},{64,96},{96,64},{128,160},{160,128},{192,224},{224,1... | collective-permute-start | bytes 786440 | tf_op jit(solution)/shard_map/ppermute | solution.py:301
  33.5 1.2 %collective-permute-done.other_ref = bf16[128,8,128]{2,1,0:T(8,128)(2,1)S(1)} collective-permute-done((bf16[128,8,128]{2,1,0:T(8,128)(2,1)S(1)}, bf16[128,8,128]{2,1,0:T(8,128)(2,1)S(1)}, u32[]{:S(2)}, u32[]{:S(2)}) %collective-permute-start) | collective-permute-done | bytes 262176 | tf_op jit(solution)/shard_map/ppermute | solution.py:301
  34.7 0.0 copy-done
  34.7 0.0 copy-start.1
  34.7 0.7 copy-done.1
  35.4 35.3 %panels.1 = (f32[384,1024]{1,0:T(8,128)}, f32[384,1024]{1,0:T(8,128)}, f32[4,1024]{1,0:T(4,128)}) custom-call(bf16[2,4,128]{2,1,0:T(4,128)(2,1)} %own_ref.1, bf16[128,8,128]{2,1,0:T(8,128)(2,1)} %copy-done, bf16[128,8,128]{2,1,0:T(8,128)(2,1)} %copy-done.1, bf16[384,128]{1,0:T(8,128)(2,1)} %landmarks_ref.1), custom_call_target="tpu_custom_call" | custom-call | tf_op jit(solution)/shard_map/panels/pallas_call | solution.py:267
Async XLA Ops:
  31.0 3.7 %copy-start = (bf16[128,8,128]{2,1,0:T(8,128)(2,1)}, bf16[128,8,128]{2,1,0:T(8,128)(2,1)S(1)}, u32[]{:S(2)}) copy-start(bf16[128,8,128]{2,1,0:T(8,128)(2,1)S(1)} %all_to_all.5.same_ref) | copy-start | bytes 786436
  31.0 3.7 %collective-permute-start = (bf16[128,8,128]{2,1,0:T(8,128)(2,1)S(1)}, bf16[128,8,128]{2,1,0:T(8,128)(2,1)S(1)}, u32[]{:S(2)}, u32[]{:S(2)}) collective-permute-start(bf16[128,8,128]{2,1,0:T(8,128)(2,1)S(1)} %all_to_all.5.same_ref), channel_id=1, source_target_pairs={{0,32},{32,0},{64,96},{96,64},{128,160},{160,128},{192,224},{224,1... | collective-permute-start | bytes 786440 | tf_op jit(solution)/shard_map/ppermute | solution.py:301
  34.7 0.7 copy-start.1

commit v3 on v2

--- a/solution.py
+++ b/solution.py
@@ -136,54 +136,52 @@
     return jnp.exp((2.0 * dot_t(left, right) - left_sq - right_sq) * (1.0 / FEAT))
 
 
-def arrange_pivots(source_ref, pivots_ref, core):
-    chips = lax.axis_size("row") // CORES
-    columns = source_ref.shape[0] // chips
-    count = columns * SUB // 2
-    row = lax.broadcasted_iota(jnp.int32, (columns // 2, SUB, FEAT), 1)
-    for y in range(chips):
-        x = source_ref[columns * y:columns * (y + 1)].astype(f32).reshape(columns // 2, 2, SUB, FEAT)
-        even, odd = x[:, 0], x[:, 1]
-        first = jnp.where(row < SUB // 2, even, pltpu.roll(odd, SUB // 2, 1))
-        second = jnp.where(row < SUB // 2, pltpu.roll(even, SUB // 2, 1), odd)
-        at = (y * CORES + core) * count
-        for base, value in ((0, first), (PANEL, second)):
-            rows = pl.ds(pl.multiple_of(base + at, count), count)
-            pivots_ref[rows, :] = value.reshape(count, FEAT).astype(bf16)
-
-
 def local_body(own_ref, same_ref, other_ref, landmarks_ref, low_ref, updated_ref, next_ref,
                panel, bottom, panel_high, panel_low, bottom_high, bottom_low, right_kernels,
-               inverse_high, inverse_low, pivots_ref, left_ref):
+               inverse_high, inverse_low, pivots_ref, left_ref, lane_squares):
     local_rows = landmarks_ref.shape[0]
     own_rows = next_ref.shape[0]
     offset = lax.axis_index(("row", "col")) * own_rows
-    core = lax.axis_index("row") % CORES
-    arrange_pivots(same_ref, pivots_ref, core)
-    arrange_pivots(other_ref, pivots_ref, 1 - core)
     left_count = left_ref.shape[0]
-    left_ref[:local_rows, :] = landmarks_ref[...]
-    padding = jnp.zeros((left_count - local_rows - own_rows, FEAT), f32)
-    left_ref[local_rows:, :] = jnp.concatenate(
-        [own_ref[1].astype(f32), padding], axis=0).astype(bf16)
-    first = pivots_ref[:PANEL, :]
-    first_lanes = squares_along_lanes(first)
     chunks = [slice(at, at + OUTER) for at in range(0, PANEL, OUTER)]
-    part = OUTER
-    bottom_chunks = [slice(at, at + part) for at in range(0, PANEL, part)]
-    bottom_chunks.append(slice(PANEL, PANEL + left_count))
+    bottom_chunks = chunks + [slice(PANEL, PANEL + left_count)]
+    chips = lax.axis_size("row") // CORES
+    columns_of_mesh = same_ref.shape[0] // chips
+    first_core = lax.axis_index("row") % CORES == 0
+
+    def arrange(y):
+        count = columns_of_mesh * SUB // 2
+        row = lax.broadcasted_iota(jnp.int32, (columns_of_mesh // 2, SUB, FEAT), 1)
+        held = slice(columns_of_mesh * y, columns_of_mesh * (y + 1))
+        same, other = same_ref[held].astype(f32), other_ref[held].astype(f32)
+        by_core = (jnp.where(first_core, same, other), jnp.where(first_core, other, same))
+        for core, x in enumerate(by_core):
+            x = x.reshape(columns_of_mesh // 2, 2, SUB, FEAT)
+            even, odd = x[:, 0], x[:, 1]
+            first = jnp.where(row < SUB // 2, even, pltpu.roll(odd, SUB // 2, 1))
+            second = jnp.where(row < SUB // 2, pltpu.roll(even, SUB // 2, 1), odd)
+            at = (y * CORES + core) * count
+            pivots_ref[at:at + count, :] = first.reshape(count, FEAT).astype(bf16)
+            pivots_ref[PANEL + at:PANEL + at + count, :] = second.reshape(count, FEAT).astype(bf16)
+
+    def arrange_left():
+        left_ref[:local_rows, :] = landmarks_ref[...]
+        padding = jnp.zeros((left_count - local_rows - own_rows, FEAT), f32)
+        left_ref[local_rows:, :] = jnp.concatenate(
+            [own_ref[1].astype(f32), padding], axis=0).astype(bf16)
 
     def panel_values(rows):
         x = pivots_ref[rows, :]
+        lane_squares[:, rows] = squares_along_lanes(x)
         width = rows.stop
-        values = kernel_values(x, squares(x), first[:width], first_lanes[:, :width])
+        values = kernel_values(x, squares(x), pivots_ref[:width, :], lane_squares[:, :width])
         row = lax.broadcasted_iota(jnp.int32, values.shape, 0) + rows.start
         column = lax.broadcasted_iota(jnp.int32, values.shape, 1)
         panel[rows, :width] = values + jnp.where(row == column, RIDGE, 0.0)
 
     def bottom_values(rows):
         x = left_ref[...] if rows.start == PANEL else pivots_ref[PANEL + rows.start:PANEL + rows.stop, :]
-        bottom[rows, :] = kernel_values(x, squares(x), first, first_lanes)
+        bottom[rows, :] = kernel_values(x, squares(x), pivots_ref[:PANEL, :], lane_squares[...])
 
     def right_values(columns):
         x = left_ref[...]
@@ -197,66 +195,107 @@
         if rows.start == PANEL:
             low_ref[:, columns] = solved[:local_rows]
 
-    def reduce(target, high, low, rows, columns):
-        done = slice(0, columns.start)
-        right = (panel_high[columns, done], panel_low[columns, done])
-        left = (high[rows, done], low[rows, done])
-        target[rows, columns] = target[rows, columns] - product(dot_t, left, right)
+    def reduce(target, high, low, rows, columns, stop, parts=False):
+        right = (panel_high[columns, :stop], panel_low[columns, :stop])
+        left = (high[rows, :stop], low[rows, :stop])
+        values = target[rows, columns] - product(dot_t, left, right)
+        if parts:
+            high[rows, columns], low[rows, columns] = split(values)
+        else:
+            target[rows, columns] = values
 
     def update(at, columns):
         left = (bottom_high[PANEL:, at], bottom_low[PANEL:, at])
         right = (bottom_high[columns, at], bottom_low[columns, at])
-        values = right_kernels[:, columns] - product(dot_t, left, right)
-        if at.stop < PANEL:
-            right_kernels[:, columns] = values
-            return
-        updated_ref[:, columns] = values[:local_rows]
+        right_kernels[:, columns] = right_kernels[:, columns] - product(dot_t, left, right)
+
+    def later(call, *operands):
+        return lambda: call(*operands)
+
+    def assemble(upper, across, lower):
+        corner = -product(dot_n, lower, split(product(dot_n, across, upper)))
+        low_half, high_half = slice(0, INNER), slice(INNER, OUTER)
+        for ref, part, up, down in zip((inverse_high, inverse_low), split(corner), upper, lower):
+            ref[low_half, low_half] = up
+            ref[low_half, high_half] = jnp.zeros((INNER, INNER), bf16)
+            ref[high_half, low_half] = part
+            ref[high_half, high_half] = down
+
+    def head_of_next(rows, left_half, right_half, upper, across):
+        solved = split(product(dot_t, split(panel[rows, left_half]), upper))
+        panel_high[rows, left_half], panel_low[rows, left_half] = solved
+        panel[rows, right_half] = panel[rows, right_half] - product(dot_t, solved, across)
+        panel[rows, rows] = panel[rows, rows] - product(dot_t, solved, solved)
+
+    def rest_of_next(rows, half, right_half, lower, top):
+        solved = split(product(dot_t, split(panel[rows, right_half]), lower))
+        panel_high[rows, right_half], panel_low[rows, right_half] = solved
+        panel[rows, half] = panel[rows, half] - product(dot_t, solved, top)
+        panel[rows, rows] = panel[rows, rows] - product(dot_t, solved, solved)
+
+    arrange(0)
+    panel_values(chunks[0])
+    carried = []
+    block = panel[:INNER, :INNER]
+    for step, columns in enumerate(chunks):
+        at, mid, end = columns.start, columns.start + INNER, columns.stop
+        left_half, right_half = slice(at, mid), slice(mid, end)
+        final = step + 1 == len(chunks)
+        work = list(carried)
+        if step == 0:
+            for y in range(1, chips):
+                work += [later(arrange, y), later(panel_values, chunks[y])]
+            work += [arrange_left]
+            work += [later(bottom_values, rows) for rows in bottom_chunks]
+            ahead = len(work)
+            work += [later(right_values, block_columns) for block_columns in chunks]
+        else:
+            before = chunks[step - 1]
+            work += [later(solve, panel, panel_high, panel_low, rows, before)
+                     for rows in chunks[step + 1:]]
+            work += [later(reduce, panel, panel_high, panel_low, rows, columns, at)
+                     for rows in chunks[step + 1:]]
+            if not final:
+                work += [later(reduce, panel, panel_high, panel_low, chunks[step + 1],
+                               chunks[step + 1], at)]
+            ahead = len(work)
+            work += [later(solve, bottom, bottom_high, bottom_low, rows, before)
+                     for rows in bottom_chunks]
+            work += [later(update, before, block_columns) for block_columns in chunks]
+            work += [later(reduce, bottom, bottom_high, bottom_low, rows, columns, at, final)
+                     for rows in bottom_chunks]
+        half = max(ahead, len(work) // 2)
+        upper = split(inverse_factor(block, work[:half]))
+        work = work[half:]
+        across = split(product(dot_t, split(panel[right_half, left_half]), upper))
+        block = panel[right_half, right_half] - product(dot_t, across, across)
+        if not final:
+            rows = chunks[step + 1]
+            work = [later(head_of_next, rows, left_half, right_half, upper, across)] + work
+        lower = split(inverse_factor(block, work))
+        carried = [later(assemble, upper, across, lower)]
+        if not final:
+            top = slice(rows.start, rows.start + INNER)
+            rest = slice(rows.start + INNER, rows.stop)
+            solved = split(product(dot_t, split(panel[top, right_half]), lower))
+            panel_high[top, right_half], panel_low[top, right_half] = solved
+            block = panel[top, top] - product(dot_t, solved, solved)
+            carried = [later(rest_of_next, rest, top, right_half, lower, solved)] + carried
+
+    assemble(upper, across, lower)
+    columns = chunks[-1]
+    inverse = (inverse_high[...], inverse_low[...])
+    solved = product(dot_t, (bottom_high[PANEL:, columns], bottom_low[PANEL:, columns]), inverse)
+    low_ref[:, columns] = solved[:local_rows]
+    left = split(product(dot_n, split(solved), inverse))
+    for rows in chunks:
+        values = right_kernels[:, rows] - product(
+            dot_t, left, (bottom_high[rows, columns], bottom_low[rows, columns]))
+        updated_ref[:, rows] = values[:local_rows]
         own = values[local_rows:local_rows + own_rows]
         row = lax.broadcasted_iota(jnp.int32, own.shape, 0) + offset
-        column = lax.broadcasted_iota(jnp.int32, own.shape, 1) + columns.start
-        next_ref[:, columns] = own + jnp.where(row == column, RIDGE, 0.0)
-
-    def later(call, *operands):
-        return lambda: call(*operands)
-
-    panel_values(chunks[0])
-    for step, columns in enumerate(chunks):
-        at, mid, end = columns.start, columns.start + INNER, columns.stop
-        work = []
-        if step == 0:
-            work += [later(panel_values, rows) for rows in chunks[1:]]
-            work += [later(bottom_values, rows) for rows in bottom_chunks]
-            work += [later(right_values, block) for block in chunks]
-        else:
-            before = chunks[step - 1]
-            reduce(panel, panel_high, panel_low, columns, columns)
-            work += [later(solve, panel, panel_high, panel_low, rows, before)
-                     for rows in chunks[step + 1:]]
-            work += [later(reduce, panel, panel_high, panel_low, rows, columns)
-                     for rows in chunks[step + 1:]]
-            work += [later(solve, bottom, bottom_high, bottom_low, rows, before)
-                     for rows in bottom_chunks]
-            work += [later(update, before, block) for block in chunks]
-            work += [later(reduce, bottom, bottom_high, bottom_low, rows, columns)
-                     for rows in bottom_chunks]
-        half = len(work) // 2
-        upper = inverse_factor(panel[at:mid, at:mid], work[:half])
-        upper_parts = split(upper)
-        across = product(dot_t, split(panel[mid:end, at:mid]), upper_parts)
-        across_parts = split(across)
-        lower = inverse_factor(
-            panel[mid:end, mid:end] - product(dot_t, across_parts, across_parts), work[half:])
-        corner = -product(dot_n, split(lower), split(product(dot_n, across_parts, upper_parts)))
-        inverse = jnp.concatenate([
-            jnp.concatenate([upper, jnp.zeros((INNER, INNER), f32)], axis=1),
-            jnp.concatenate([corner, lower], axis=1)], axis=0)
-        inverse_high[...], inverse_low[...] = split(inverse)
-        if step + 1 < len(chunks):
-            solve(panel, panel_high, panel_low, chunks[step + 1], columns)
-    for rows in bottom_chunks:
-        solve(bottom, bottom_high, bottom_low, rows, chunks[-1])
-    for block in chunks:
-        update(chunks[-1], block)
+        column = lax.broadcasted_iota(jnp.int32, own.shape, 1) + rows.start
+        next_ref[:, rows] = own + jnp.where(row == column, RIDGE, 0.0)
 
 
 def local_call(own, same, other, landmarks):
@@ -283,6 +322,7 @@
             pltpu.VMEM((OUTER, OUTER), bf16),
             pltpu.VMEM((2 * PANEL, FEAT), bf16),
             pltpu.VMEM((left_count, FEAT), bf16),
+            pltpu.VMEM((1, PANEL), f32),
         ],
         compiler_params=pltpu.CompilerParams(vmem_limit_bytes=56 * 1024 * 1024),
         name="panels",

time: 70.8 us -> 70.3 us (level)
  no operation moved by 1% of the time
where the time goes in v3:
time: 70.3 us; the launch traced here: 70.2 us
  Pallas kernels  34.8 us (50%)
  blocking collectives  29.6 us (42%)
  starting transfers between devices  2.56 us (4%)
  local copies, waits for them, and re-layouts  1.43 us (2%)
  waiting for transfers between devices  1.16 us (2%)
    pallas_call x1, Pallas kernels, local_call(): pl.pallas_call(local_body, out_shape=(jax.ShapeDtypeStruct((local_rows, P...  34.8 us
    all_to_all x1, blocking collectives, body(): lax.all_to_all(copies, ('row', 'col'), 0, 0, axis_index_groups=groups, ti...  29.6 us
    ppermute x1, starting transfers between devices, body(): other = lax.ppermute(same, 'row', [(i, i ^ 1) for i in range(rows)])  2.56 us
  transfers between devices with their start and end apart: 1, of which 1 were waited for; matrix products, arithmetic and copies ran while one was open for 0% of the time, Pallas kernels for 0%

profile of v3, /device:TPU:1, one launch (start us, length us, event | category | flops | bytes accessed | tf_op | source)
XLA Modules:
  0.0 70.2 jit_solution(15512925368069983235)
XLA Ops:
  0.6 0.7 %broadcast_in_dim.8 = bf16[128,8,128]{2,1,0:T(8,128)(2,1)S(1)} broadcast(bf16[8,128]{1,0:T(8,128)(2,1)} %bitcast.1), dimensions={1,2} | broadcast | bytes 264192 | tf_op jit(solution)/shard_map/broadcast_in_dim | solution.py:339
  1.4 29.6 %all_to_all.5.same_ref = bf16[128,8,128]{2,1,0:T(8,128)(2,1)S(1)} all-to-all(bf16[128,8,128]{2,1,0:T(8,128)(2,1)S(1)} %broadcast_in_dim.8), channel_id=1, replica_groups={{0,1,2,3,4,5,6,7,8,9,10,11,12,13,14,15,16,17,18,19,20,21,22,23,24,25,26..., dimensions={0} | all-to-all | bytes 524288 | tf_op jit(solution)/shard_map/all_to_all | solution.py:340
  31.0 0.0 copy-start
  31.0 2.6 %collective-permute-start = (bf16[128,8,128]{2,1,0:T(8,128)(2,1)S(1)}, bf16[128,8,128]{2,1,0:T(8,128)(2,1)S(1)}, u32[]{:S(2)}, u32[]{:S(2)}) collective-permute-start(bf16[128,8,128]{2,1,0:T(8,128)(2,1)S(1)} %all_to_all.5.same_ref), channel_id=1, source_target_pairs={{0,32},{32,0},{64,96},{96,64},{128,160},{160,128},{192,224},{224,1... | collective-permute-start | bytes 786440 | tf_op jit(solution)/shard_map/ppermute | solution.py:341
  33.5 1.2 %collective-permute-done.other_ref = bf16[128,8,128]{2,1,0:T(8,128)(2,1)S(1)} collective-permute-done((bf16[128,8,128]{2,1,0:T(8,128)(2,1)S(1)}, bf16[128,8,128]{2,1,0:T(8,128)(2,1)S(1)}, u32[]{:S(2)}, u32[]{:S(2)}) %collective-permute-start) | collective-permute-done | bytes 262176 | tf_op jit(solution)/shard_map/ppermute | solution.py:341
  34.7 0.0 copy-done
  34.7 0.0 copy-start.1
  34.7 0.7 %copy-done.1 = bf16[128,8,128]{2,1,0:T(8,128)(2,1)} copy-done((bf16[128,8,128]{2,1,0:T(8,128)(2,1)}, bf16[128,8,128]{2,1,0:T(8,128)(2,1)S(1)}, u32[]{:S(2)}) %copy-start.1) | copy-done | bytes 262168
  35.4 34.8 %panels.1 = (f32[384,1024]{1,0:T(8,128)}, f32[384,1024]{1,0:T(8,128)}, f32[4,1024]{1,0:T(4,128)}) custom-call(bf16[2,4,128]{2,1,0:T(4,128)(2,1)} %own_ref.1, bf16[128,8,128]{2,1,0:T(8,128)(2,1)} %copy-done, bf16[128,8,128]{2,1,0:T(8,128)(2,1)} %copy-done.1, bf16[384,128]{1,0:T(8,128)(2,1)} %landmarks_ref.1), custom_call_target="tpu_custom_call" | custom-call | tf_op jit(solution)/shard_map/panels/pallas_call | solution.py:306
Async XLA Ops:
  31.0 3.7 %copy-start = (bf16[128,8,128]{2,1,0:T(8,128)(2,1)}, bf16[128,8,128]{2,1,0:T(8,128)(2,1)S(1)}, u32[]{:S(2)}) copy-start(bf16[128,8,128]{2,1,0:T(8,128)(2,1)S(1)} %all_to_all.5.same_ref) | copy-start | bytes 786436
  31.0 3.7 %collective-permute-start = (bf16[128,8,128]{2,1,0:T(8,128)(2,1)S(1)}, bf16[128,8,128]{2,1,0:T(8,128)(2,1)S(1)}, u32[]{:S(2)}, u32[]{:S(2)}) collective-permute-start(bf16[128,8,128]{2,1,0:T(8,128)(2,1)S(1)} %all_to_all.5.same_ref), channel_id=1, source_target_pairs={{0,32},{32,0},{64,96},{96,64},{128,160},{160,128},{192,224},{224,1... | collective-permute-start | bytes 786440 | tf_op jit(solution)/shard_map/ppermute | solution.py:341
  34.7 0.7 %copy-start.1 = (bf16[128,8,128]{2,1,0:T(8,128)(2,1)}, bf16[128,8,128]{2,1,0:T(8,128)(2,1)S(1)}, u32[]{:S(2)}) copy-start(bf16[128,8,128]{2,1,0:T(8,128)(2,1)S(1)} %collective-permute-done.other_ref) | copy-start | bytes 786436

commit v4 on v3

--- a/solution.py
+++ b/solution.py
@@ -136,9 +136,10 @@
     return jnp.exp((2.0 * dot_t(left, right) - left_sq - right_sq) * (1.0 / FEAT))
 
 
-def local_body(own_ref, same_ref, other_ref, landmarks_ref, low_ref, updated_ref, next_ref,
+def local_body(own_ref, same_ref, other_ref, landmarks_ref, low_out, updated_out, next_ref,
                panel, bottom, panel_high, panel_low, bottom_high, bottom_low, right_kernels,
-               inverse_high, inverse_low, pivots_ref, left_ref, lane_squares):
+               inverse_high, inverse_low, pivots_ref, left_ref, lane_squares, low_ref, updated_ref,
+               sent):
     local_rows = landmarks_ref.shape[0]
     own_rows = next_ref.shape[0]
     offset = lax.axis_index(("row", "col")) * own_rows
@@ -148,6 +149,14 @@
     chips = lax.axis_size("row") // CORES
     columns_of_mesh = same_ref.shape[0] // chips
     first_core = lax.axis_index("row") % CORES == 0
+
+    copies = []
+
+    def send(source, target, columns):
+        copy = pltpu.make_async_copy(
+            source.at[:, columns], target.at[:, columns], sent.at[len(copies)])
+        copy.start()
+        copies.append(copy)
 
     def arrange(y):
         count = columns_of_mesh * SUB // 2
@@ -194,6 +203,7 @@
         high[rows, columns], low[rows, columns] = split(solved)
         if rows.start == PANEL:
             low_ref[:, columns] = solved[:local_rows]
+            send(low_ref, low_out, columns)
 
     def reduce(target, high, low, rows, columns, stop, parts=False):
         right = (panel_high[columns, :stop], panel_low[columns, :stop])
@@ -287,15 +297,19 @@
     inverse = (inverse_high[...], inverse_low[...])
     solved = product(dot_t, (bottom_high[PANEL:, columns], bottom_low[PANEL:, columns]), inverse)
     low_ref[:, columns] = solved[:local_rows]
+    send(low_ref, low_out, columns)
     left = split(product(dot_n, split(solved), inverse))
     for rows in chunks:
         values = right_kernels[:, rows] - product(
             dot_t, left, (bottom_high[rows, columns], bottom_low[rows, columns]))
         updated_ref[:, rows] = values[:local_rows]
+        send(updated_ref, updated_out, rows)
         own = values[local_rows:local_rows + own_rows]
         row = lax.broadcasted_iota(jnp.int32, own.shape, 0) + offset
         column = lax.broadcasted_iota(jnp.int32, own.shape, 1) + rows.start
         next_ref[:, rows] = own + jnp.where(row == column, RIDGE, 0.0)
+    for copy in copies:
+        copy.wait()
 
 
 def local_call(own, same, other, landmarks):
@@ -323,7 +337,15 @@
             pltpu.VMEM((2 * PANEL, FEAT), bf16),
             pltpu.VMEM((left_count, FEAT), bf16),
             pltpu.VMEM((1, PANEL), f32),
+            pltpu.VMEM((local_rows, PANEL), f32),
+            pltpu.VMEM((local_rows, PANEL), f32),
+            pltpu.SemaphoreType.DMA((2 * PANEL // OUTER,)),
         ],
+        out_specs=(
+            pl.BlockSpec(memory_space=pl.ANY),
+            pl.BlockSpec(memory_space=pl.ANY),
+            pl.BlockSpec(memory_space=pltpu.VMEM),
+        ),
         compiler_params=pltpu.CompilerParams(vmem_limit_bytes=56 * 1024 * 1024),
         name="panels",
     )(own, same, other, landmarks)

time: 70.3 us -> 71 us (level)
  no operation moved by 1% of the time
where the time goes in v4:
time: 71 us; the launch traced here: 70.9 us
  Pallas kernels  35.3 us (50%)
  blocking collectives  29.6 us (42%)
  starting transfers between devices  2.56 us (4%)
  local copies, waits for them, and re-layouts  1.43 us (2%)
  waiting for transfers between devices  1.16 us (2%)
  between operations  0.84 us (1%)
    pallas_call x1, Pallas kernels, local_call(): pl.pallas_call(local_body, out_shape=(jax.ShapeDtypeStruct((local_rows, P...  35.3 us
    all_to_all x1, blocking collectives, body(): lax.all_to_all(copies, ('row', 'col'), 0, 0, axis_index_groups=groups, ti...  29.6 us
    ppermute x1, starting transfers between devices, body(): other = lax.ppermute(same, 'row', [(i, i ^ 1) for i in range(rows)])  2.56 us
  transfers between devices with their start and end apart: 1, of which 1 were waited for; matrix products, arithmetic and copies ran while one was open for 0% of the time, Pallas kernels for 0%

profile of v4, /device:TPU:1, one launch (start us, length us, event | category | flops | bytes accessed | tf_op | source)
XLA Modules:
  0.0 70.9 jit_solution(5667208733946223236)
XLA Ops:
  0.6 0.7 %broadcast_in_dim.8 = bf16[128,8,128]{2,1,0:T(8,128)(2,1)S(1)} broadcast(bf16[8,128]{1,0:T(8,128)(2,1)} %bitcast.1), dimensions={1,2} | broadcast | bytes 264192 | tf_op jit(solution)/shard_map/broadcast_in_dim | solution.py:361
  1.4 29.6 %all_to_all.5.same_ref = bf16[128,8,128]{2,1,0:T(8,128)(2,1)S(1)} all-to-all(bf16[128,8,128]{2,1,0:T(8,128)(2,1)S(1)} %broadcast_in_dim.8), channel_id=1, replica_groups={{0,1,2,3,4,5,6,7,8,9,10,11,12,13,14,15,16,17,18,19,20,21,22,23,24,25,26..., dimensions={0} | all-to-all | bytes 524288 | tf_op jit(solution)/shard_map/all_to_all | solution.py:362
  31.0 0.0 copy-start
  31.0 2.6 %collective-permute-start = (bf16[128,8,128]{2,1,0:T(8,128)(2,1)S(1)}, bf16[128,8,128]{2,1,0:T(8,128)(2,1)S(1)}, u32[]{:S(2)}, u32[]{:S(2)}) collective-permute-start(bf16[128,8,128]{2,1,0:T(8,128)(2,1)S(1)} %all_to_all.5.same_ref), channel_id=1, source_target_pairs={{0,32},{32,0},{64,96},{96,64},{128,160},{160,128},{192,224},{224,1... | collective-permute-start | bytes 786440 | tf_op jit(solution)/shard_map/ppermute | solution.py:363
  33.5 1.2 %collective-permute-done.other_ref = bf16[128,8,128]{2,1,0:T(8,128)(2,1)S(1)} collective-permute-done((bf16[128,8,128]{2,1,0:T(8,128)(2,1)S(1)}, bf16[128,8,128]{2,1,0:T(8,128)(2,1)S(1)}, u32[]{:S(2)}, u32[]{:S(2)}) %collective-permute-start) | collective-permute-done | bytes 262176 | tf_op jit(solution)/shard_map/ppermute | solution.py:363
  34.7 0.0 copy-done
  34.7 0.0 copy-start.1
  34.7 0.7 copy-done.1
  35.4 35.3 %panels.1 = (f32[384,1024]{1,0:T(8,128)}, f32[384,1024]{1,0:T(8,128)}, f32[4,1024]{1,0:T(4,128)}) custom-call(bf16[2,4,128]{2,1,0:T(4,128)(2,1)} %own_ref.1, bf16[128,8,128]{2,1,0:T(8,128)(2,1)} %copy-done, bf16[128,8,128]{2,1,0:T(8,128)(2,1)} %copy-done.1, bf16[384,128]{1,0:T(8,128)(2,1)} %landmarks_ref.1), custom_call_target="tpu_custom_call" | custom-call | tf_op jit(solution)/shard_map/panels/pallas_call | solution.py:320
Async XLA Ops:
  31.0 3.7 %copy-start = (bf16[128,8,128]{2,1,0:T(8,128)(2,1)}, bf16[128,8,128]{2,1,0:T(8,128)(2,1)S(1)}, u32[]{:S(2)}) copy-start(bf16[128,8,128]{2,1,0:T(8,128)(2,1)S(1)} %all_to_all.5.same_ref) | copy-start | bytes 786436
  31.0 3.7 %collective-permute-start = (bf16[128,8,128]{2,1,0:T(8,128)(2,1)S(1)}, bf16[128,8,128]{2,1,0:T(8,128)(2,1)S(1)}, u32[]{:S(2)}, u32[]{:S(2)}) collective-permute-start(bf16[128,8,128]{2,1,0:T(8,128)(2,1)S(1)} %all_to_all.5.same_ref), channel_id=1, source_target_pairs={{0,32},{32,0},{64,96},{96,64},{128,160},{160,128},{192,224},{224,1... | collective-permute-start | bytes 786440 | tf_op jit(solution)/shard_map/ppermute | solution.py:363
  34.7 0.7 copy-start.1
